TPU v7x, 256 devices: a whole 4x4x8 slice. The times are simulated.
256 devices in a mesh: shard: 16 (over y, x), grp: 16 (over z, core).
Axes of the slice: x: 4, y: 4, z: 8, core: 2. Of those that a mesh axis runs over, the one named last changes fastest.
Arguments:
- embedding: bfloat16 [65536, 768], P(('shard', 'grp'))
- cluster_id: int32 [65536], P(('shard', 'grp')), may hold values from 0 to 63, as said below
- member_order: int32 [65536], P(('shard', 'grp')), may hold values from 0 to 65535, each once
Outputs:
- nearest_earlier: float32 [65536], P(('shard', 'grp'))
Inputs may be any that keep to these rules, and one draw needn't show every extreme that they name: `cluster_id`: the rows of cluster c are kept by owner shard c // 4. Of the rows of one device, at most 40 belong to one owner shard, and exactly 40 to some owner shard. Across the devices that share an index along grp, exactly 256 rows belong to each owner shard.
All inputs are finite; a program needn't handle non-finite values.
Results may differ from a plain program's by a relative error of at most 0.00068.
Values may be sent and summed in bfloat16 or wider, within the bound.
A program may use at most 64 MiB of HBM per device.

v0:
```python
import jax
import jax.numpy as jnp
from jax import lax
from jax.sharding import PartitionSpec as P

CLUST_OWN = 4


def scorer(queries, query_cluster, query_rank):

    def absorb(running, blocks, first_row):
        key_rows, key_cluster, key_rank = blocks
        scores = lax.dot_general(
            queries, key_rows, (((1,), (1,)), ((), ())), preferred_element_type=jnp.float32
        )
        allowed = (query_cluster[:, None] == key_cluster[None, :]) & (
            key_rank[None, :] < query_rank[:, None]
        )
        return jnp.maximum(running, jnp.max(jnp.where(allowed, scores, -1.0), axis=1))

    return absorb


def per_device(embedding, cluster_id, member_order):
    shards = lax.axis_size("shard")
    row_dev = embedding.shape[0]
    width = embedding.shape[1]
    capacity = 5 * row_dev // (2 * shards)
    widened = embedding.astype(jnp.float32)
    normed = (
        widened * lax.rsqrt(jnp.sum(widened * widened, axis=1, keepdims=True) + 1e-06)
    ).astype(jnp.bfloat16)
    owner_shard = cluster_id // CLUST_OWN
    onehot = (owner_shard[:, None] == jnp.arange(shards, dtype=jnp.int32)[None, :]).astype(
        jnp.int32
    )
    before = jnp.cumsum(onehot, axis=0) - onehot
    slot_index = jnp.sum(before * onehot, axis=1)
    target = owner_shard * capacity + slot_index
    send_rows = jnp.zeros((shards * capacity, width), jnp.bfloat16).at[target].set(normed)
    send_cluster = jnp.full((shards * capacity,), -1, jnp.int32).at[target].set(cluster_id)
    send_rank = jnp.zeros((shards * capacity,), jnp.int32).at[target].set(member_order)
    got_rows, got_cluster, got_rank = (
        lax.all_to_all(
            send_rows.reshape(shards, capacity, width),
            "shard",
            split_axis=0,
            concat_axis=0,
            tiled=True,
        ),
        lax.all_to_all(
            send_cluster.reshape(shards, capacity), "shard", split_axis=0, concat_axis=0, tiled=True
        ),
        lax.all_to_all(
            send_rank.reshape(shards, capacity), "shard", split_axis=0, concat_axis=0, tiled=True
        ),
    )
    member_rows = got_rows.reshape(shards * capacity, width)
    member_cluster = got_cluster.reshape(shards * capacity)
    member_rank = got_rank.reshape(shards * capacity)
    start_max = jnp.full((shards * capacity,), -1.0, jnp.float32)
    absorb = scorer(member_rows, member_cluster, member_rank)
    best_sim = absorb(
        start_max,
        (
            lax.all_gather(member_rows, "grp", axis=0, tiled=True),
            lax.all_gather(member_cluster, "grp", axis=0, tiled=True),
            lax.all_gather(member_rank, "grp", axis=0, tiled=True),
        ),
        jnp.int32(0),
    )
    returned = lax.all_to_all(
        best_sim.reshape(shards, capacity), "shard", split_axis=0, concat_axis=0, tiled=True
    )
    return returned.reshape(shards * capacity)[target]


def solution(mesh):
    in_specs = (P(("shard", "grp"), None), P(("shard", "grp")), P(("shard", "grp")))
    out_specs = P(("shard", "grp"))
    return jax.shard_map(
        per_device, mesh=mesh, in_specs=in_specs, out_specs=out_specs, check_vma=False
    )
```

profile of v0, /device:TPU:1, one launch (start us, length us, event | category | flops | bytes accessed | tf_op | source)
XLA Modules:
  0.0 166.9 jit_solution(17130259277363811312)
XLA Ops:
  6.5 0.0 all-gather.4.cloned.1.call-start
  6.5 0.7 fusion.16
  7.2 0.7 and_select_fusion
  7.9 1.2 fusion
  9.1 0.6 reduce-window.6
  9.7 0.2 slice_reduce_fusion
  9.9 0.1 fusion.8
  10.0 0.7 compare_select_fusion
  10.7 2.5 %scatter_custom_fusion.2 = bf16[640,768]{1,0:T(8,128)(2,1)S(1)} fusion(s32[256]{0:T(256)S(1)} %compare_select_fusion, bf16[]{:T(256)} %constant.34.clone.1, bf16[256,768]{1,0:T(8,128)(2,1)} %param.3, f32[256]{0:T(256)S(1)} %add_rsqrt_fusion), kind=kCustom, calls=%fused_computation.9 | custom fusion | flops 589824 | bytes 1377282 | tf_op jit(solution)/shard_map/scatter | solution.py:40
  13.2 23.1 %all_to_all.29 = bf16[16,40,768]{2,1,0:T(8,128)(2,1)} all-to-all(bf16[16,40,768]{2,1,0:T(8,128)(2,1)S(1)} %bitcast.34), channel_id=1, replica_groups=mesh['shard'=16,'grp'=16] {'shard'}, dimensions={0} | all-to-all | bytes 1966080 | tf_op jit(solution)/shard_map/all_to_all | solution.py:44
  36.3 0.0 all-gather.4.cloned.1.call-update
  36.3 1.6 scatter_custom_fusion
  37.9 0.7 all_to_all.19
  38.6 3.5 %all-to-all-start = ((s32[16,1,40]{2,1,0:T(1,128)}), s32[16,1,40]{2,1,0:T(1,128)S(1)}, u32[]{:S(2)}, u32[]{:S(2)}) async-start(s32[16,1,40]{2,1,0:T(1,128)} %all_to_all.19), calls=%async_computation | async-start | bytes 16384 | tf_op jit(solution)/shard_map/all_to_all | solution.py:51
  42.1 1.6 scatter_custom_fusion.1
  43.6 0.7 all_to_all.21
  44.3 4.1 %all-to-all-done = s32[16,1,40]{2,1,0:T(1,128)S(1)} async-done(((s32[16,1,40]{2,1,0:T(1,128)}), s32[16,1,40]{2,1,0:T(1,128)S(1)}, u32[]{:S(2)}, u32[]{:S(2)}) %all-to-all-start) | async-done | bytes 2592 | tf_op jit(solution)/shard_map/all_to_all | solution.py:51
  48.4 3.5 %all-to-all-start.1 = ((s32[16,1,40]{2,1,0:T(1,128)}), s32[16,1,40]{2,1,0:T(1,128)S(1)}, u32[]{:S(2)}, u32[]{:S(2)}) async-start(s32[16,1,40]{2,1,0:T(1,128)} %all_to_all.21), calls=%async_computation.1 | async-start | bytes 16384 | tf_op jit(solution)/shard_map/all_to_all | solution.py:54
  51.9 0.1 reshape.109
  52.0 0.5 broadcast.70
  52.5 0.7 reduce.16
  53.2 0.1 eq.45
  53.3 5.0 %all-to-all-done.1 = s32[16,1,40]{2,1,0:T(1,128)S(1)} async-done(((s32[16,1,40]{2,1,0:T(1,128)}), s32[16,1,40]{2,1,0:T(1,128)S(1)}, u32[]{:S(2)}, u32[]{:S(2)}) %all-to-all-start.1) | async-done | bytes 2592 | tf_op jit(solution)/shard_map/all_to_all | solution.py:54
  58.2 0.1 reshape.69
  58.3 0.7 reduce.15
  59.0 0.1 reshape.111
  59.1 23.8 %all-gather.1 = s32[16,1,640]{2,1,0:T(1,128)S(1)} all-gather(s32[1,1,640]{2,1,0:T(1,128)S(1)} %reshape.111), channel_id=1, replica_groups=mesh['shard'=16,'grp'=16] {'grp'}, dimensions={0}, use_global_device_ids=true | all-gather | bytes 43520 | tf_op jit(solution)/shard_map/all_gather | solution.py:68
  82.9 14.6 %all-gather = s32[16,1,640]{2,1,0:T(1,128)S(1)} all-gather(s32[1,1,640]{2,1,0:T(1,128)S(1)} %reshape.109), channel_id=1, replica_groups=mesh['shard'=16,'grp'=16] {'grp'}, dimensions={0}, use_global_device_ids=true | all-gather | bytes 43520 | tf_op jit(solution)/shard_map/all_gather | solution.py:67
  97.5 30.4 %all-gather.4.cloned.1.call-done = bf16[10240,768]{1,0:T(8,128)(2,1)} async-done(((bf16[640,768]{1,0:T(8,128)(2,1)}), bf16[10240,768]{1,0:T(8,128)(2,1)}) %all-gather.4.cloned.1.call-update) | async-done | bytes 15728656 | tf_op jit(solution)/shard_map/all_gather | solution.py:66
  128.0 15.2 %select_reduce_fusion = f32[640]{0:T(1024)S(1)} fusion(bf16[640,768]{1,0:T(8,128)(2,1)} %bitcast.33, bf16[10240,768]{1,0:T(8,128)(2,1)} %all-gather.4.cloned.1.call-done, s32[10240]{0:T(1024)S(1)} %bitcast.37, s32[10240]{0:T(1024)S(1)} %bitcast.38, s32[640]{0:T(1024)S(1)} %reshape.69, s32[640]{0:T(1024)S(1)} %eq.45), kind=kOutput, calls=%fused_computation.4 | convolution fusion | flops 10099096576 | bytes 16801280 | tf_op jit(solution)/shard_map/dot_general | solution.py:13
  143.2 0.7 max_broadcast_in_dim.15
  143.9 6.5 %all-to-all-start.3 = ((f32[16,1,40]{2,1,0:T(1,128)}), f32[16,1,40]{2,1,0:T(1,128)S(1)}, u32[]{:S(2)}, u32[]{:S(2)}) async-start(f32[16,1,40]{2,1,0:T(1,128)} %max_broadcast_in_dim.15), calls=%async_computation.3 | async-start | bytes 16384 | tf_op jit(solution)/shard_map/all_to_all | solution.py:72
  150.5 6.4 %all-to-all-done.3 = f32[16,1,40]{2,1,0:T(1,128)S(1)} async-done(((f32[16,1,40]{2,1,0:T(1,128)}), f32[16,1,40]{2,1,0:T(1,128)S(1)}, u32[]{:S(2)}, u32[]{:S(2)}) %all-to-all-start.3) | async-done | bytes 2592 | tf_op jit(solution)/shard_map/all_to_all | solution.py:72
  156.9 0.5 broadcast.72
  157.4 0.7 reduce.17
  158.1 0.1 reshape.72
  158.1 1.9 %gather_fusion = f32[256]{0:T(256)} fusion(f32[640]{0:T(1024)S(1)} %reshape.72, s32[1024]{0:T(1024)S(1)} %pad_clamp_fusion), kind=kCustom, calls=%fused_computation | custom fusion | bytes 3072 | tf_op jit(solution)/shard_map/gather | solution.py:75
  (6 shorter events, 0.1 us)
Async XLA Ops:
  6.5 121.4 %all-gather.4.cloned.1.call-start = ((), (), s32[]{:S(2)}) async-start(), calls=%async_computation.4 | async-start | bytes 16711680 | tf_op jit(solution)/shard_map/all_gather | solution.py:66
  38.6 9.8 %all-to-all-start = ((s32[16,1,40]{2,1,0:T(1,128)}), s32[16,1,40]{2,1,0:T(1,128)S(1)}, u32[]{:S(2)}, u32[]{:S(2)}) async-start(s32[16,1,40]{2,1,0:T(1,128)} %all_to_all.19), calls=%async_computation | async-start | bytes 16384 | tf_op jit(solution)/shard_map/all_to_all | solution.py:51
  48.4 9.8 %all-to-all-start.1 = ((s32[16,1,40]{2,1,0:T(1,128)}), s32[16,1,40]{2,1,0:T(1,128)S(1)}, u32[]{:S(2)}, u32[]{:S(2)}) async-start(s32[16,1,40]{2,1,0:T(1,128)} %all_to_all.21), calls=%async_computation.1 | async-start | bytes 16384 | tf_op jit(solution)/shard_map/all_to_all | solution.py:54
  143.9 12.9 %all-to-all-start.3 = ((f32[16,1,40]{2,1,0:T(1,128)}), f32[16,1,40]{2,1,0:T(1,128)S(1)}, u32[]{:S(2)}, u32[]{:S(2)}) async-start(f32[16,1,40]{2,1,0:T(1,128)} %max_broadcast_in_dim.15), calls=%async_computation.3 | async-start | bytes 16384 | tf_op jit(solution)/shard_map/all_to_all | solution.py:72
Sparse Core Ops, SparseCore 0:
  36.4 91.5 all-gather.3
where the time goes:
time: 167 us
  blocking collectives  61.5 us (37%)
  waiting for transfers between devices  45.9 us (27%)
  matrix products  15.2 us (9%)
  starting transfers between devices  13.5 us (8%)
  between operations  13.5 us (8%)
  local copies, waits for them, and re-layouts  8.74 us (5%)
  other arithmetic  8.48 us (5%)
    all_gather x1, waiting for transfers between devices, per_device(): lax.all_gather(member_rows, 'grp', axis=0, tiled=True)  30.4 us
    all_gather x1, blocking collectives, per_device(): lax.all_gather(member_rank, 'grp', axis=0, tiled=True)  23.8 us
    all_to_all x1, blocking collectives, per_device(): lax.all_to_all(send_rows.reshape(shards, capacity, width), 'shard', split...  23.1 us
    dot_general x1, matrix products, absorb(): lax.dot_general(queries, key_rows, (((1,), (1,)), ((), ())), preferred_el...  15.2 us
    all_gather x1, blocking collectives, per_device(): lax.all_gather(member_cluster, 'grp', axis=0, tiled=True)  14.6 us
    all_to_all x1, starting transfers between devices, per_device(): lax.all_to_all(best_sim.reshape(shards, capacity), 'shard', split_axis=0,...  6.54 us
    all_to_all x1, waiting for transfers between devices, per_device(): lax.all_to_all(best_sim.reshape(shards, capacity), 'shard', split_axis=0,...  6.39 us
    all_to_all x1, waiting for transfers between devices, per_device(): lax.all_to_all(send_rank.reshape(shards, capacity), 'shard', split_axis=0...  4.98 us
  transfers between devices with their start and end apart: 4, of which 4 were waited for; matrix products, arithmetic and copies ran while one was open for 3% of the time, Pallas kernels for 0%

commit v1 on v0

v1 whole, which is shorter than its diff:
```python
import functools

import jax
import jax.numpy as jnp
from jax import lax
from jax.experimental import pallas as pl
from jax.experimental.pallas import tpu as pltpu
from jax.sharding import PartitionSpec as P

MESH = pl.DeviceIdType.MESH
HIGHEST = lax.Precision.HIGHEST
CLUST_OWN = 4
SIDE = 4
RANKS = 65536

T0, TP1, TM1, TP2, TM2, U0, UM1, UM2 = range(8)
PP1, PM1, PP2, PU0, PUM1 = range(5)


def iota(shape, dim):
    return lax.broadcasted_iota(jnp.int32, shape, dim)


def one_hot(cond, dtype=jnp.bfloat16):
    return jnp.where(cond, 1.0, 0.0).astype(dtype)


def dot_nt(a, b, precision=None):
    return lax.dot_general(
        a, b, (((1,), (1,)), ((), ())), preferred_element_type=jnp.float32, precision=precision
    )


def dot_nn(a, b, precision=None):
    return lax.dot_general(
        a, b, (((1,), (0,)), ((), ())), preferred_element_type=jnp.float32, precision=precision
    )


def kernel(
    shards,
    capacity,
    emb_ref,
    cid_ref,
    rank_ref,
    out_ref,
    send_buf,
    recv_buf,
    blk,
    meta_send,
    meta_recv,
    zmeta,
    kcol,
    part_send,
    part_recv,
    ret_send,
    ret_recv,
    xy_send,
    xy_recv,
    meta_ssem,
    meta_rsem,
    z_send,
    z_recv,
    zm_send,
    zm_recv,
    p_send,
    p_recv,
    r_send,
    r_recv,
):
    row_dev = emb_ref.shape[0]
    chunks = blk.shape[1]
    width = blk.shape[3]
    half = width // 2
    me = lax.axis_index("shard")
    grp = lax.axis_index("grp")
    y, x = me // SIDE, me % SIDE
    z, core = grp // 2, grp % 2
    n_z = lax.axis_size("grp") // 2

    def xy_dev(k, sign):
        dy, dx = k // SIDE, k % SIDE
        py = (y + sign * dy + SIDE) % SIDE
        px = (x + sign * dx + SIDE) % SIDE
        return (py * SIDE + px, grp)

    def z_dev(dz, other):
        pc = 1 - core if other else core
        return (me, ((z + dz + n_z) % n_z) * 2 + pc)

    barrier = pltpu.get_barrier_semaphore()
    for k in range(1, shards):
        pl.semaphore_signal(barrier, inc=1, device_id=xy_dev(k, 1), device_id_type=MESH)
    column = [(d, o) for d in (-2, -1, 0, 1, 2) for o in (False, True) if (d, o) != (0, False)]
    for d, o in column:
        pl.semaphore_signal(barrier, inc=1, device_id=z_dev(d, o), device_id_type=MESH)

    def remote(src, dst, ssem, rsem, dev):
        copy = pltpu.make_async_remote_copy(
            src_ref=src, dst_ref=dst, send_sem=ssem, recv_sem=rsem, device_id=dev, device_id_type=MESH
        )
        copy.start()

    def arrived(ref, sem):
        pltpu.make_async_copy(ref, ref, sem).wait()

    cid = cid_ref[...]
    owner = cid // CLUST_OWN
    rel = ((owner // SIDE - y + SIDE) % SIDE) * SIDE + (owner % SIDE - x + SIDE) % SIDE
    is_owner = iota((shards, row_dev), 0) == rel
    earlier = one_hot(iota((row_dev, row_dev), 0) < iota((row_dev, row_dev), 1))
    before = dot_nn(one_hot(is_owner), earlier)
    slot = jnp.sum(jnp.where(is_owner, before, 0.0), axis=0, keepdims=True).astype(jnp.int32)
    target = rel * capacity + slot
    pack = one_hot(iota((shards * capacity, row_dev), 0) == target)

    key_own = (cid * RANKS + rank_ref[...] + 1).astype(jnp.float32)
    row_no = (iota((1, row_dev), 1) + 1).astype(jnp.float32)
    lane_k = iota((128, row_dev), 0)
    meta = dot_nt(
        jnp.where(is_owner, key_own, 0.0), one_hot(lane_k == slot, jnp.float32), HIGHEST
    ) + dot_nt(
        jnp.where(is_owner, row_no, 0.0), one_hot(lane_k == slot + 64, jnp.float32), HIGHEST
    )
    meta_recv[0] = meta[0:1]
    for k in range(1, shards):
        meta_send[k] = meta[k : k + 1]

    wide = emb_ref[...].astype(jnp.float32)
    normed = (
        wide * lax.rsqrt(jnp.sum(wide * wide, axis=1, keepdims=True) + 1e-06)
    ).astype(jnp.bfloat16)

    def pack_chunk(q):
        rows = dot_nn(pack, normed[:, q * width : (q + 1) * width])
        rows = rows.reshape(shards, capacity, width)
        rows = jnp.concatenate([rows[:, :, :half], rows[:, :, half:]], axis=1).astype(jnp.bfloat16)
        recv_buf[q, 0] = rows[0]
        send_buf[q, 1:] = rows[1:]

    def send_chunk(q):
        for k in range(1, shards):
            remote(
                send_buf.at[q, k], recv_buf.at[q, k], xy_send.at[q], xy_recv.at[q], xy_dev(k, 1)
            )

    pack_chunk(0)
    pl.semaphore_wait(barrier, shards - 1 + len(column))
    for k in range(1, shards):
        remote(meta_send.at[k], meta_recv.at[k], meta_ssem, meta_rsem, xy_dev(k, 1))
    send_chunk(0)
    for q in range(1, chunks):
        pack_chunk(q)
        send_chunk(q)

    arrived(meta_recv.at[pl.ds(1, shards - 1)], meta_rsem)
    got = meta_recv[...].reshape(shards, 128)
    lanes = iota((shards, 128), 1)
    count = jnp.sum(jnp.where((got > 0.0) & (lanes < 64), 1.0, 0.0), axis=1, keepdims=True)
    lower = iota((shards, shards), 1) < iota((shards, shards), 0)
    count_row = jnp.sum(
        jnp.where(iota((shards, shards), 0) == iota((shards, shards), 1), count, 0.0),
        axis=0,
        keepdims=True,
    )
    offset = jnp.sum(jnp.where(lower, count_row, 0.0), axis=1, keepdims=True)
    offset_i = offset.astype(jnp.int32)
    count_i = count.astype(jnp.int32)

    places = shards * 2 * capacity
    inner = iota((shards, places), 1) - iota((shards, places), 0) * (2 * capacity)

    def place(h):
        k = inner - h * capacity
        good = (k >= 0) & (k < jnp.minimum(count_i, capacity))
        return jnp.sum(jnp.where(good, offset_i + k + 1, 0), axis=0, keepdims=True) - 1

    pos = iota((row_dev, places), 0)
    gather = jnp.concatenate([one_hot(pos == place(0)), one_hot(pos == place(1))], axis=0)

    member = iota((shards, row_dev), 1)
    from_src = (member >= offset_i) & (member < offset_i + count_i)
    within = iota((1, row_dev), 1) - jnp.sum(
        jnp.where(from_src, offset_i, 0), axis=0, keepdims=True
    )
    got_t = jnp.concatenate([got, jnp.zeros((128 - shards, 128), jnp.float32)], axis=0).T
    from_pad = jnp.concatenate(
        [one_hot(from_src, jnp.float32), jnp.zeros((128 - shards, row_dev), jnp.float32)], axis=0
    )
    spread = dot_nn(got_t, from_pad, HIGHEST)
    key_row = jnp.sum(jnp.where(lane_k == within, spread, 0.0), axis=0, keepdims=True) - 1.0
    home_row = jnp.sum(jnp.where(lane_k == within + 64, spread, 0.0), axis=0, keepdims=True) - 1.0
    zmeta[T0] = key_row
    for slot_no, d, o in (
        (TP1, -1, False),
        (TM1, 1, False),
        (TP2, -2, False),
        (TM2, 2, False),
        (U0, 0, True),
        (UM1, 1, True),
        (UM2, 2, True),
    ):
        remote(zmeta.at[T0], zmeta.at[slot_no], zm_send, zm_recv, z_dev(d, o))

    def compact(q):
        arrived(recv_buf.at[q, pl.ds(1, shards - 1)], xy_recv.at[q])
        both = dot_nn(gather, recv_buf[q].reshape(places, half))
        blk[T0, q] = jnp.concatenate([both[:row_dev], both[row_dev:]], axis=1).astype(jnp.bfloat16)

    def z_copy(src_slot, dst_slot, q, d, o):
        remote(
            blk.at[src_slot, q],
            blk.at[dst_slot, q],
            z_send.at[dst_slot, q],
            z_recv.at[dst_slot, q],
            z_dev(d, o),
        )

    def z_wait(slot_no, q):
        arrived(blk.at[slot_no, q], z_recv.at[slot_no, q])

    def send_own(q):
        z_copy(T0, TM1, q, 1, False)
        z_copy(T0, TP1, q, -1, False)
        z_copy(T0, U0, q, 0, True)

    def forward(q):
        z_wait(TM1, q)
        z_copy(TM1, TM2, q, 1, False)
        z_copy(TM1, UM1, q, 0, True)
        z_wait(TP1, q)
        z_copy(TP1, TP2, q, -1, False)

    for q in range(chunks):
        compact(q)
        send_own(q)
        if q:
            forward(q - 1)
    forward(chunks - 1)

    arrived(zmeta.at[pl.ds(1, 7)], zm_recv)
    keys = zmeta[...].reshape(8, row_dev)
    eye = one_hot(iota((row_dev, row_dev), 0) == iota((row_dev, row_dev), 1), jnp.float32)
    keys_t = dot_nt(eye, keys, HIGHEST)
    for b in range(8):
        kcol[b] = jnp.broadcast_to(keys_t[:, b : b + 1], (row_dev, row_dev))
    first_key = jnp.floor(keys * (1.0 / RANKS)) * RANKS

    def best(query, key_slots, running=None):
        for ks in key_slots:
            scores = dot_nt(blk[ks, 0], blk[query, 0])
            for q in range(1, chunks):
                scores += dot_nt(blk[ks, q], blk[query, q])
            col = kcol[ks]
            allowed = (col < keys[query : query + 1]) & (col >= first_key[query : query + 1])
            top = jnp.max(jnp.where(allowed, scores, -1.0), axis=0, keepdims=True)
            running = top if running is None else jnp.maximum(running, top)
        return running

    def send_part(p, value, d, o):
        part_send[p] = value
        remote(part_send.at[p], part_recv.at[p], p_send, p_recv, z_dev(d, o))

    for q in range(chunks):
        z_wait(U0, q)
    mine = best(T0, (T0, U0, TP1))
    send_part(PU0, best(U0, (TP1,)), 0, True)
    for q in range(chunks):
        z_wait(TM2, q)
        z_copy(TM2, UM2, q, 0, True)
    for q in range(chunks):
        z_wait(UM1, q)
    send_part(PP1, best(TP1, (T0, U0, TM1, UM1)), 1, False)
    early_m1 = best(TM1, (TP1,))
    early_um1 = best(UM1, (TP1,))
    for q in range(chunks):
        z_wait(TP2, q)
    send_part(PM1, best(TM1, (TP2,), early_m1), -1, False)
    send_part(PUM1, best(UM1, (TP2,), early_um1), -1, True)
    late = best(TP2, (TM1, UM1, TM2))
    for q in range(chunks):
        z_wait(UM2, q)
    send_part(PP2, best(TP2, (UM2,), late), 2, False)

    arrived(part_recv, p_recv)
    mine = jnp.maximum(mine, jnp.max(part_recv[...].reshape(5, row_dev), axis=0, keepdims=True))
    back = dot_nt(
        jnp.where(from_src, mine, 0.0),
        one_hot(iota((row_dev, row_dev), 0) == home_row.astype(jnp.int32), jnp.float32),
        HIGHEST,
    )
    ret_recv[0] = back[0:1]
    for k in range(1, shards):
        ret_send[k] = back[k : k + 1]
    for k in range(1, shards):
        remote(ret_send.at[k], ret_recv.at[k], r_send, r_recv, xy_dev(k, -1))
    arrived(ret_recv.at[pl.ds(1, shards - 1)], r_recv)
    out_ref[...] = jnp.sum(ret_recv[...].reshape(shards, row_dev), axis=0, keepdims=True)

    arrived(meta_send.at[pl.ds(1, shards - 1)], meta_ssem)
    for q in range(chunks):
        arrived(send_buf.at[q, pl.ds(1, shards - 1)], xy_send.at[q])
        for b in range(1, 8):
            arrived(blk.at[b, q], z_send.at[b, q])
    arrived(zmeta.at[pl.ds(1, 7)], zm_send)
    arrived(part_send, p_send)
    arrived(ret_send.at[pl.ds(1, shards - 1)], r_send)


def per_device(embedding, cluster_id, member_order):
    shards = lax.axis_size("shard")
    row_dev, depth = embedding.shape
    capacity = 5 * row_dev // (2 * shards)
    width = 256
    chunks = depth // width
    dma = pltpu.SemaphoreType.DMA
    out = pl.pallas_call(
        functools.partial(kernel, shards, capacity),
        out_shape=jax.ShapeDtypeStruct((1, row_dev), jnp.float32),
        in_specs=[pl.BlockSpec(memory_space=pltpu.VMEM)] * 3,
        out_specs=pl.BlockSpec(memory_space=pltpu.VMEM),
        scratch_shapes=[
            pltpu.VMEM((chunks, shards, 2 * capacity, width // 2), jnp.bfloat16),
            pltpu.VMEM((chunks, shards, 2 * capacity, width // 2), jnp.bfloat16),
            pltpu.VMEM((8, chunks, row_dev, width), jnp.bfloat16),
            pltpu.VMEM((shards, 1, 128), jnp.float32),
            pltpu.VMEM((shards, 1, 128), jnp.float32),
            pltpu.VMEM((8, 1, row_dev), jnp.float32),
            pltpu.VMEM((8, row_dev, row_dev), jnp.float32),
            pltpu.VMEM((5, 1, row_dev), jnp.float32),
            pltpu.VMEM((5, 1, row_dev), jnp.float32),
            pltpu.VMEM((shards, 1, row_dev), jnp.float32),
            pltpu.VMEM((shards, 1, row_dev), jnp.float32),
            dma((chunks,)),
            dma((chunks,)),
            dma,
            dma,
            dma((8, chunks)),
            dma((8, chunks)),
            dma,
            dma,
            dma,
            dma,
            dma,
            dma,
        ],
        compiler_params=pltpu.CompilerParams(
            collective_id=0, has_side_effects=True, vmem_limit_bytes=40 * 2**20
        ),
    )(embedding, cluster_id.reshape(1, row_dev), member_order.reshape(1, row_dev))
    return out.reshape(row_dev)


def solution(mesh):
    in_specs = (P(("shard", "grp"), None), P(("shard", "grp")), P(("shard", "grp")))
    out_specs = P(("shard", "grp"))
    return jax.shard_map(
        per_device, mesh=mesh, in_specs=in_specs, out_specs=out_specs, check_vma=False
    )
```

time: 167 us -> 51 us (0.31)
  blocking collectives: 61.5 us -> 0 us
  Pallas kernels: 0 us -> 47.8 us
  waiting for transfers between devices: 45.9 us -> 0 us
  matrix products: 15.2 us -> 0 us
  starting transfers between devices: 13.5 us -> 0 us
  between operations: 13.5 us -> 0.01 us
  other arithmetic: 8.48 us -> 0 us
  local copies, waits for them, and re-layouts: 8.74 us -> 2.25 us
    pallas_call x0 -> x1, Pallas kernels: none -> 47.8 us  [per_device(): pl.pallas_call(functools.partial(kernel, shards, capacity), out_shape=jax...]
    all_gather x2 -> x0, blocking collectives: 38.5 us -> none  [the longest x1 23.8 us: per_device(): lax.all_gather(member_rank, 'grp', axis=0, tiled=True)]
    all_gather x1 -> x0, waiting for transfers between devices: 30.4 us -> none  [per_device(): lax.all_gather(member_rows, 'grp', axis=0, tiled=True)]
    all_to_all x1 -> x0, blocking collectives: 23.1 us -> none  [per_device(): lax.all_to_all(send_rows.reshape(shards, capacity, width), 'shard', split...]
    all_to_all x3 -> x0, waiting for transfers between devices: 15.5 us -> none  [the longest x1 6.39 us: per_device(): lax.all_to_all(best_sim.reshape(shards, capacity), 'shard', split_axis=0,...]
    dot_general x1 -> x0, matrix products: 15.2 us -> none  [absorb(): lax.dot_general(queries, key_rows, (((1,), (1,)), ((), ())), preferred_el...]
    all_to_all x3 -> x0, starting transfers between devices: 13.5 us -> none  [the longest x1 6.54 us: per_device(): lax.all_to_all(best_sim.reshape(shards, capacity), 'shard', split_axis=0,...]
    scatter x2 -> x0, local copies, waits for them, and re-layouts: 3.12 us -> none  [the longest x1 1.56 us: per_device(): jnp.full((shards * capacity,), -1, jnp.int32).at[target].set(cluster_id)]
  transfers between devices with their start and end apart: 4 -> 0, of which waited for: 4 -> 0; matrix products, arithmetic and copies ran while one was open for 3% -> 0% of each run, Pallas kernels for 0% -> 0%
where the time goes in v1:
time: 51 us; the launch traced here: 50.1 us
  Pallas kernels  47.8 us (94%)
  local copies, waits for them, and re-layouts  2.25 us (4%)
    pallas_call x1, Pallas kernels, per_device(): pl.pallas_call(functools.partial(kernel, shards, capacity), out_shape=jax...  47.8 us
    unnamed x7, local copies, waits for them, and re-layouts  2.25 us

profile of v1, /device:TPU:1, one launch (start us, length us, event | category | flops | bytes accessed | tf_op | source)
XLA Modules:
  0.0 50.1 jit_solution(8289124386995820637)
XLA Ops:
  0.0 0.0 copy-start.2
  0.0 0.0 copy-start.1
  0.0 0.7 %copy-done.2 = s32[256]{0:T(256)S(1)} copy-done((s32[256]{0:T(256)S(1)}, s32[256]{0:T(256)}, u32[]{:S(2)}) %copy-start.2) | copy-done | bytes 1048
  0.7 0.0 copy-done.1
  0.7 0.0 copy-start
  0.7 1.0 %copy-done = bf16[256,768]{1,0:T(8,128)(2,1)S(1)} copy-done((bf16[256,768]{1,0:T(8,128)(2,1)S(1)}, bf16[256,768]{1,0:T(8,128)(2,1)}, u32[]{:S(2)}) %copy-start) | copy-done | bytes 393240
  1.7 47.8 %shard_map.37 = f32[1,256]{1,0:T(1,128)S(1)} custom-call(bf16[256,768]{1,0:T(8,128)(2,1)S(1)} %copy-done, s32[1,256]{1,0:T(1,128)S(1)} %bitcast.4, s32[1,256]{1,0:T(1,128)S(1)} %bitcast.5), custom_call_target="tpu_custom_call" | custom-call | tf_op jit(solution)/shard_map/pallas_call | solution.py:317
  49.5 0.6 %copy.5 = f32[256]{0:T(256)} copy(f32[256]{0:T(256)S(1)} %bitcast.3) | data formatting | bytes 2048
Async XLA Ops:
  0.0 0.7 %copy-start.2 = (s32[256]{0:T(256)S(1)}, s32[256]{0:T(256)}, u32[]{:S(2)}) copy-start(s32[256]{0:T(256)} %param.5) | copy-start | bytes 3076
  0.0 0.7 %copy-start.1 = (s32[256]{0:T(256)S(1)}, s32[256]{0:T(256)}, u32[]{:S(2)}) copy-start(s32[256]{0:T(256)} %param.4) | copy-start | bytes 3076
  0.7 1.0 %copy-start = (bf16[256,768]{1,0:T(8,128)(2,1)S(1)}, bf16[256,768]{1,0:T(8,128)(2,1)}, u32[]{:S(2)}) copy-start(bf16[256,768]{1,0:T(8,128)(2,1)} %emb_ref.1) | copy-start | bytes 1179652

commit v2 on v1

v2 whole, which is shorter than its diff:
```python
import functools

import jax
import jax.numpy as jnp
from jax import lax
from jax.experimental import pallas as pl
from jax.experimental.pallas import tpu as pltpu
from jax.sharding import PartitionSpec as P

MESH = pl.DeviceIdType.MESH
HIGHEST = lax.Precision.HIGHEST
CLUST_OWN = 4
SIDE = 4
RANKS = 65536
UNIT = 128
PREPARE = 2
PLAN = (1, 1, 2, 2)

T0, TP1, TM1, TP2, TM2, U0, UM1, UM2 = range(8)
PP1, PM1, PP2, PU0, PUM1 = range(5)
DIRECT = ((TP1, TM1),)


def iota(shape, dim):
    return lax.broadcasted_iota(jnp.int32, shape, dim)


def one_hot(cond, dtype=jnp.bfloat16):
    return jnp.where(cond, 1.0, 0.0).astype(dtype)


def dot_nt(a, b, precision=None):
    return lax.dot_general(
        a, b, (((1,), (1,)), ((), ())), preferred_element_type=jnp.float32, precision=precision
    )


def dot_nn(a, b, precision=None):
    return lax.dot_general(
        a, b, (((1,), (0,)), ((), ())), preferred_element_type=jnp.float32, precision=precision
    )


def dot_whole(a, selector):
    rows = a.shape[0]
    pieces = []
    for _ in range(3):
        pieces.append(a.astype(jnp.bfloat16))
        a = a - pieces[-1].astype(jnp.float32)
    out = dot_nt(jnp.concatenate(pieces, axis=0), selector)
    return out[:rows] + out[rows : 2 * rows] + out[2 * rows :]


def kernel(shards, capacity, plan, emb_hbm, cid_hbm, rank_hbm, out_ref, *refs):
    n = len(plan)
    m = n + len(DIRECT)
    send_buf, recv_buf, refs = refs[:m], refs[m : 2 * m], refs[2 * m :]
    (
        emb_ref,
        cid_ref,
        rank_ref,
        blk,
        acc,
        meta_send,
        meta_recv,
        zmeta,
        raw,
        raw_target,
        counts,
        kcol,
        part_send,
        part_recv,
        ret_send,
        ret_recv,
        in_sem,
        xy_send,
        xy_recv,
        meta_ssem,
        meta_rsem,
        z_send,
        z_recv,
        zm_send,
        zm_recv,
        raw_ssem,
        raw_rsem,
        rt_send,
        rt_recv,
        c_send,
        c_recv,
        p_send,
        p_recv,
        r_send,
        r_recv,
    ) = refs
    row_dev = emb_ref.shape[0]
    padded = -(-capacity // 16) * 16
    first = [sum(plan[:q]) for q in range(n + 1)]
    last = first[n] - 1 if DIRECT else first[n]
    direct = [b for pair in DIRECT for b in pair]
    me = lax.axis_index("shard")
    grp = lax.axis_index("grp")
    y, x = me // SIDE, me % SIDE
    z, core = grp // 2, grp % 2
    n_z = lax.axis_size("grp") // 2

    loads = [
        pltpu.make_async_copy(src, dst, in_sem.at[a])
        for a, (src, dst) in enumerate(
            ((cid_hbm, cid_ref), (rank_hbm, rank_ref), (emb_hbm, emb_ref))
        )
    ]
    for load in loads:
        load.start()

    def xy_dev(k, sign):
        dy, dx = k // SIDE, k % SIDE
        py = (y + sign * dy + SIDE) % SIDE
        px = (x + sign * dx + SIDE) % SIDE
        return (py * SIDE + px, grp)

    def z_dev(dz, other):
        pc = 1 - core if other else core
        return (me, ((z + dz + n_z) % n_z) * 2 + pc)

    barrier = pltpu.get_barrier_semaphore()
    for k in range(1, shards):
        pl.semaphore_signal(barrier, inc=1, device_id=xy_dev(k, 1), device_id_type=MESH)
    column = [(d, o) for d in (-2, -1, 0, 1, 2) for o in (False, True) if (d, o) != (0, False)]
    for d, o in column:
        pl.semaphore_signal(barrier, inc=1, device_id=z_dev(d, o), device_id_type=MESH)

    def remote(src, dst, ssem, rsem, dev):
        copy = pltpu.make_async_remote_copy(
            src_ref=src, dst_ref=dst, send_sem=ssem, recv_sem=rsem, device_id=dev, device_id_type=MESH
        )
        copy.start()

    def arrived(ref, sem):
        pltpu.make_async_copy(ref, ref, sem).wait()

    loads[0].wait()
    loads[1].wait()
    cid = cid_ref[...]
    owner = cid // CLUST_OWN
    rel = ((owner // SIDE - y + SIDE) % SIDE) * SIDE + (owner % SIDE - x + SIDE) % SIDE
    is_owner = iota((shards, row_dev), 0) == rel
    earlier = one_hot(iota((row_dev, row_dev), 0) < iota((row_dev, row_dev), 1))
    before = dot_nn(one_hot(is_owner), earlier)
    slot = jnp.sum(jnp.where(is_owner, before, 0.0), axis=0, keepdims=True).astype(jnp.int32)
    target = rel * padded + slot
    pack = one_hot(iota((shards * padded, row_dev), 0) == target)

    key_own = (cid * RANKS + rank_ref[...] + 1).astype(jnp.float32)
    row_no = (iota((1, row_dev), 1) + 1).astype(jnp.float32)
    lane_k = iota((128, row_dev), 0)
    meta = dot_whole(jnp.where(is_owner, key_own, 0.0), one_hot(lane_k == slot)) + dot_nt(
        jnp.where(is_owner, row_no, 0.0).astype(jnp.bfloat16), one_hot(lane_k == slot + 64)
    )
    meta_recv[0] = meta[0:1]
    for k in range(1, shards):
        meta_send[k] = meta[k : k + 1]

    loads[2].wait()
    wide = emb_ref[...].astype(jnp.float32)
    normed = (
        wide * lax.rsqrt(jnp.sum(wide * wide, axis=1, keepdims=True) + 1e-06)
    ).astype(jnp.bfloat16)

    if DIRECT:
        raw[T0] = normed[:, last * UNIT :]
        raw_target[T0] = target.astype(jnp.float32)
    neighbours = [bd for bd in ((TP1, -1), (TM1, 1), (TP2, -2), (TM2, 2)) if bd[0] in direct]

    def pack_chunk(q):
        rows = dot_nn(pack, normed[:, first[q] * UNIT : first[q + 1] * UNIT])
        rows = rows.reshape(shards, padded, plan[q] * UNIT)
        if plan[q] == 2:
            rows = jnp.concatenate(
                [rows[:, :capacity, :UNIT], rows[:, :capacity, UNIT:]], axis=1
            )
        rows = rows.astype(jnp.bfloat16)
        recv_buf[q][0] = rows[0]
        send_buf[q][1:] = rows[1:]

    def send_chunk(q):
        for k in range(1, shards):
            remote(
                send_buf[q].at[k], recv_buf[q].at[k], xy_send.at[q], xy_recv.at[q], xy_dev(k, 1)
            )

    pack_chunk(0)
    pl.semaphore_wait(barrier, shards - 1 + len(column))
    for k in range(1, shards):
        remote(meta_send.at[k], meta_recv.at[k], meta_ssem, meta_rsem, xy_dev(k, 1))
    send_chunk(0)
    for b, d in neighbours:
        remote(raw_target.at[T0], raw_target.at[b], rt_send, rt_recv, z_dev(d, False))
        remote(raw.at[T0], raw.at[b], raw_ssem.at[b], raw_rsem.at[b], z_dev(d, False))
    for q in range(1, n):
        pack_chunk(q)
        send_chunk(q)

    def pack_direct(e):
        halves = []
        for b in DIRECT[e]:
            arrived(raw.at[b], raw_rsem.at[b])
            to = raw_target[b].astype(jnp.int32)
            rows = dot_nn(one_hot(iota((shards * padded, row_dev), 0) == to), raw[b])
            halves.append(rows.reshape(shards, padded, UNIT)[:, :capacity])
        rows = jnp.concatenate(halves, axis=1).astype(jnp.bfloat16)
        recv_buf[n + e][0] = rows[0]
        send_buf[n + e][1:] = rows[1:]
        send_chunk(n + e)

    arrived(meta_recv.at[pl.ds(1, shards - 1)], meta_rsem)
    got = meta_recv[...].reshape(shards, 128)
    lanes = iota((shards, 128), 1)
    count = jnp.sum(jnp.where((got > 0.0) & (lanes < 64), 1.0, 0.0), axis=1, keepdims=True)
    lower = iota((shards, shards), 1) < iota((shards, shards), 0)
    count_row = jnp.sum(
        jnp.where(iota((shards, shards), 0) == iota((shards, shards), 1), count, 0.0),
        axis=0,
        keepdims=True,
    )
    offset = jnp.sum(jnp.where(lower, count_row, 0.0), axis=1, keepdims=True).astype(jnp.int32)
    count = count.astype(jnp.int32)

    def place(units, h, offset=offset, count=count):
        rows = padded if units == 1 else units * capacity
        k = iota((shards, shards * rows), 1) - iota((shards, shards * rows), 0) * rows - h * capacity
        good = (k >= 0) & (k < count)
        where_to = jnp.sum(jnp.where(good, offset + k + 1, 0), axis=0, keepdims=True) - 1
        return one_hot(iota((row_dev, shards * rows), 0) == where_to)

    gathers = {}

    def compact(q):
        units = plan[q]
        if units not in gathers:
            gathers[units] = jnp.concatenate([place(units, h) for h in range(units)], axis=0)
        arrived(recv_buf[q].at[pl.ds(1, shards - 1)], xy_recv.at[q])
        rows = recv_buf[q][...]
        out = dot_nn(gathers[units], rows.reshape(rows.shape[0] * rows.shape[1], UNIT))
        blk[T0, first[q] : first[q + 1]] = out.reshape(units, row_dev, UNIT).astype(jnp.bfloat16)

    def direct_places(e):
        places = []
        for h, b in enumerate(DIRECT[e]):
            packed = counts[b][:, :1].astype(jnp.int32)
            places.append(place(2, h, packed % 1024, packed // 1024))
        return jnp.concatenate(places, axis=0)

    def compact_direct(e):
        arrived(recv_buf[n + e].at[pl.ds(1, shards - 1)], xy_recv.at[n + e])
        rows = recv_buf[n + e][...]
        out = dot_nn(
            direct_gather[e], rows.reshape(rows.shape[0] * rows.shape[1], UNIT)
        ).astype(jnp.bfloat16)
        for h, b in enumerate(DIRECT[e]):
            blk[b, last] = out[h * row_dev : (h + 1) * row_dev]

    def z_copy(src_slot, dst_slot, u, d, o):
        remote(
            blk.at[src_slot, u],
            blk.at[dst_slot, u],
            z_send.at[dst_slot, u],
            z_recv.at[dst_slot, u],
            z_dev(d, o),
        )

    def z_wait(slot_no, u):
        arrived(blk.at[slot_no, u], z_recv.at[slot_no, u])

    def units_of(q):
        return range(first[q], first[q + 1])

    def send_own(q):
        for u in units_of(q):
            if u == last:
                continue
            z_copy(T0, TM1, u, 1, False)
            z_copy(T0, TP1, u, -1, False)
        for u in units_of(q):
            z_copy(T0, U0, u, 0, True)

    def forward(q):
        for u in units_of(q):
            if u == last:
                continue
            z_wait(TM1, u)
            z_copy(TM1, TM2, u, 1, False)
            z_copy(TM1, UM1, u, 0, True)
            z_wait(TP1, u)
            z_copy(TP1, TP2, u, -1, False)

    compact(0)
    send_own(0)

    member = iota((shards, row_dev), 1)
    from_src = (member >= offset) & (member < offset + count)
    within = iota((1, row_dev), 1) - jnp.sum(jnp.where(from_src, offset, 0), axis=0, keepdims=True)
    got_t = jnp.concatenate([got, jnp.zeros((128 - shards, 128), jnp.float32)], axis=0).T
    from_pad = jnp.concatenate(
        [one_hot(from_src, jnp.float32), jnp.zeros((128 - shards, row_dev), jnp.float32)], axis=0
    )
    spread = dot_nn(got_t, from_pad, HIGHEST)
    key_row = jnp.sum(jnp.where(lane_k == within, spread, 0.0), axis=0, keepdims=True) - 1.0
    home_row = jnp.sum(jnp.where(lane_k == within + 64, spread, 0.0), axis=0, keepdims=True) - 1.0
    counts[T0] = jnp.broadcast_to((offset + 1024 * count).astype(jnp.float32), (shards, 128))
    for b, d in neighbours:
        remote(counts.at[T0], counts.at[b], c_send, c_recv, z_dev(d, False))
    zmeta[T0] = key_row
    for slot_no, d, o in (
        (TP1, -1, False),
        (TM1, 1, False),
        (TP2, -2, False),
        (TM2, 2, False),
        (U0, 0, True),
        (UM1, 1, True),
        (UM2, 2, True),
    ):
        remote(zmeta.at[T0], zmeta.at[slot_no], zm_send, zm_recv, z_dev(d, o))

    if DIRECT:
        arrived(raw_target.at[pl.ds(1, len(direct))], rt_recv)
    for q in range(1, n):
        compact(q)
        send_own(q)
        if q <= len(DIRECT):
            pack_direct(q - 1)
        forward(q - 1)
        if q == PREPARE:
            home = one_hot(iota((row_dev, row_dev), 0) == home_row.astype(jnp.int32))
            arrived(zmeta.at[pl.ds(1, 7)], zm_recv)
            keys = zmeta[...].reshape(8, row_dev)
            eye = one_hot(iota((row_dev, row_dev), 0) == iota((row_dev, row_dev), 1), jnp.float32)
            keys_t = dot_nt(eye, keys, HIGHEST)
            for b in range(8):
                kcol[b] = jnp.broadcast_to(keys_t[:, b : b + 1], (row_dev, 128))
            first_key = jnp.floor(keys * (1.0 / RANKS)) * RANKS
            if DIRECT:
                arrived(counts.at[pl.ds(1, len(direct))], c_recv)
            direct_gather = [direct_places(e) for e in range(len(DIRECT))]
    forward(n - 1)
    if DIRECT:
        compact_direct(0)
        z_copy(TM1, UM1, last, 0, True)
        if TM2 not in direct:
            z_copy(TM1, TM2, last, 1, False)
            z_copy(TP1, TP2, last, -1, False)

    def scores(query, key, start, stop):
        total = None
        for u in range(start, stop, 2):
            take = range(u, min(u + 2, stop))
            a = jnp.concatenate([blk[key, v] for v in take], axis=1)
            b = jnp.concatenate([blk[query, v] for v in take], axis=1)
            term = dot_nt(a, b)
            total = term if total is None else total + term
        return total

    def top(query, key, total):
        col = jnp.concatenate([kcol[key]] * (row_dev // 128), axis=1)
        allowed = (col < keys[query : query + 1]) & (col >= first_key[query : query + 1])
        return jnp.max(jnp.where(allowed, total, -1.0), axis=0, keepdims=True)

    def best(query, key_slots):
        running = None
        for key in key_slots:
            found = top(query, key, scores(query, key, 0, first[n]))
            running = found if running is None else jnp.maximum(running, found)
        return running

    def send_part(p, value, d, o):
        part_send[p] = value
        remote(part_send.at[p], part_recv.at[p], p_send, p_recv, z_dev(d, o))

    all_units = range(first[n])
    tail = first[n] - 2

    def pass_on(units):
        for u in units:
            z_wait(TM2, u)
            z_copy(TM2, UM2, u, 0, True)

    pass_on(range(first[n - 2]))
    for u in all_units:
        z_wait(U0, u)
    mine = best(T0, (T0, U0, TP1))
    send_part(PU0, best(U0, (TP1,)), 0, True)
    early_p1 = best(TP1, (T0, U0, TM1))
    early_m1 = best(TM1, (TP1,))
    for u in all_units:
        z_wait(UM1, u)
    send_part(PP1, jnp.maximum(early_p1, best(TP1, (UM1,))), 1, False)
    early_um1 = best(UM1, (TP1,))
    pass_on(range(first[n - 2], tail))
    if len(DIRECT) > 1:
        compact_direct(1)
        z_copy(TM2, UM2, last, 0, True)

    for u in range(tail):
        z_wait(TP2, u)
    pairs = ((TM1, TP2), (UM1, TP2), (TP2, TM1), (TP2, UM1), (TP2, TM2), (TP2, UM2))
    for a, (query, key) in enumerate(pairs):
        if key == UM2:
            for u in range(tail):
                z_wait(UM2, u)
        acc[a] = scores(query, key, 0, tail)

    def finish(a):
        query, key = pairs[a]
        return top(query, key, acc[a] + scores(query, key, tail, first[n]))

    by_z = range(tail, last if TM2 in direct else first[n])
    pass_on(by_z)
    for u in by_z:
        z_wait(TP2, u)
    send_part(PM1, jnp.maximum(early_m1, finish(0)), -1, False)
    send_part(PUM1, jnp.maximum(early_um1, finish(1)), -1, True)
    late = jnp.maximum(jnp.maximum(finish(2), finish(3)), finish(4))
    for u in range(tail, first[n]):
        z_wait(UM2, u)
    send_part(PP2, jnp.maximum(late, finish(5)), 2, False)

    arrived(part_recv, p_recv)
    mine = jnp.maximum(mine, jnp.max(part_recv[...].reshape(5, row_dev), axis=0, keepdims=True))
    back = dot_whole(jnp.where(from_src, mine, 0.0), home)
    ret_recv[0] = back[0:1]
    for k in range(1, shards):
        ret_send[k] = back[k : k + 1]
    for k in range(1, shards):
        remote(ret_send.at[k], ret_recv.at[k], r_send, r_recv, xy_dev(k, -1))
    arrived(ret_recv.at[pl.ds(1, shards - 1)], r_recv)
    out_ref[...] = jnp.sum(ret_recv[...].reshape(shards, row_dev), axis=0, keepdims=True)

    arrived(meta_send.at[pl.ds(1, shards - 1)], meta_ssem)
    for q in range(m):
        arrived(send_buf[q].at[pl.ds(1, shards - 1)], xy_send.at[q])
    for u in all_units:
        for b in range(1, 8):
            if u == last and (b in direct):
                continue
            arrived(blk.at[b, u], z_send.at[b, u])
    for b, _ in neighbours:
        arrived(raw.at[b], raw_ssem.at[b])
    if DIRECT:
        arrived(raw_target.at[pl.ds(1, len(direct))], rt_send)
    if DIRECT:
        arrived(counts.at[pl.ds(1, len(direct))], c_send)
    arrived(zmeta.at[pl.ds(1, 7)], zm_send)
    arrived(part_send, p_send)
    arrived(ret_send.at[pl.ds(1, shards - 1)], r_send)


def per_device(embedding, cluster_id, member_order):
    shards = lax.axis_size("shard")
    row_dev, depth = embedding.shape
    capacity = 5 * row_dev // (2 * shards)
    padded = -(-capacity // 16) * 16
    plan = PLAN
    n = len(plan)
    dma = pltpu.SemaphoreType.DMA
    vmem = pltpu.VMEM
    bf16, f32, i32 = jnp.bfloat16, jnp.float32, jnp.int32
    messages = [
        vmem((shards, padded if units == 1 else units * capacity, UNIT), bf16)
        for units in plan + (2,) * len(DIRECT)
    ]
    out = pl.pallas_call(
        functools.partial(kernel, shards, capacity, plan),
        out_shape=jax.ShapeDtypeStruct((1, row_dev), f32),
        in_specs=[pl.BlockSpec(memory_space=pltpu.HBM)] * 3,
        out_specs=pl.BlockSpec(memory_space=vmem),
        scratch_shapes=messages
        + messages
        + [
            vmem((row_dev, depth), bf16),
            vmem((1, row_dev), i32),
            vmem((1, row_dev), i32),
            vmem((8, depth // UNIT, row_dev, UNIT), bf16),
            vmem((6, row_dev, row_dev), f32),
            vmem((shards, 1, 128), f32),
            vmem((shards, 1, 128), f32),
            vmem((8, 1, row_dev), f32),
            vmem((5, row_dev, UNIT), bf16),
            vmem((5, 1, row_dev), f32),
            vmem((5, shards, 128), f32),
            vmem((8, row_dev, 128), f32),
            vmem((5, 1, row_dev), f32),
            vmem((5, 1, row_dev), f32),
            vmem((shards, 1, row_dev), f32),
            vmem((shards, 1, row_dev), f32),
            dma((3,)),
            dma((n + len(DIRECT),)),
            dma((n + len(DIRECT),)),
            dma,
            dma,
            dma((8, depth // UNIT)),
            dma((8, depth // UNIT)),
            dma,
            dma,
            dma((5,)),
            dma((5,)),
            dma,
            dma,
            dma,
            dma,
            dma,
            dma,
            dma,
            dma,
        ],
        compiler_params=pltpu.CompilerParams(
            collective_id=0, has_side_effects=True, vmem_limit_bytes=215 * 2**18
        ),
    )(embedding, cluster_id.reshape(1, row_dev), member_order.reshape(1, row_dev))
    return out.reshape(row_dev)


def solution(mesh):
    in_specs = (P(("shard", "grp"), None), P(("shard", "grp")), P(("shard", "grp")))
    out_specs = P(("shard", "grp"))
    return jax.shard_map(
        per_device, mesh=mesh, in_specs=in_specs, out_specs=out_specs, check_vma=False
    )
```

time: 51 us -> 46.9 us (0.920)
  Pallas kernels: 47.8 us -> 45.1 us
  local copies, waits for them, and re-layouts: 2.25 us -> 1.26 us
    pallas_call x1, Pallas kernels: 47.8 us -> 45.1 us  [per_device(): pl.pallas_call(functools.partial(kernel, shards, capacity, plan), out_sha...]
    unnamed x7 -> x5, local copies, waits for them, and re-layouts: 2.25 us -> 1.26 us
where the time goes in v2:
time: 46.9 us; the launch traced here: 46.4 us
  Pallas kernels  45.1 us (96%)
  local copies, waits for them, and re-layouts  1.26 us (3%)
    pallas_call x1, Pallas kernels, per_device(): pl.pallas_call(functools.partial(kernel, shards, capacity, plan), out_sha...  45.1 us
    unnamed x5, local copies, waits for them, and re-layouts  1.26 us

profile of v2, /device:TPU:1, one launch (start us, length us, event | category | flops | bytes accessed | tf_op | source)
XLA Modules:
  0.0 46.4 jit_solution(12795717747165274533)
XLA Ops:
  0.0 0.0 copy-start.1
  0.0 0.0 copy-start
  0.0 0.7 %copy-done.1 = s32[256]{0:T(256)S(1)} copy-done((s32[256]{0:T(256)S(1)}, s32[256]{0:T(256)}, u32[]{:S(2)}) %copy-start.1) | copy-done | bytes 1048
  0.7 0.0 copy-done
  0.7 45.1 %shard_map.37 = f32[1,256]{1,0:T(1,128)S(1)} custom-call(bf16[256,768]{1,0:T(8,128)(2,1)} %emb_hbm.1, s32[1,256]{1,0:T(1,128)S(1)} %bitcast.4, s32[1,256]{1,0:T(1,128)S(1)} %bitcast.5), custom_call_target="tpu_custom_call" | custom-call | tf_op jit(solution)/shard_map/pallas_call | solution.py:470
  45.8 0.6 %copy.5 = f32[256]{0:T(256)} copy(f32[256]{0:T(256)S(1)} %bitcast.3) | data formatting | bytes 2048
Async XLA Ops:
  0.0 0.7 %copy-start.1 = (s32[256]{0:T(256)S(1)}, s32[256]{0:T(256)}, u32[]{:S(2)}) copy-start(s32[256]{0:T(256)} %param.5) | copy-start | bytes 3076
  0.0 0.7 %copy-start = (s32[256]{0:T(256)S(1)}, s32[256]{0:T(256)}, u32[]{:S(2)}) copy-start(s32[256]{0:T(256)} %param.4) | copy-start | bytes 3076

commit v3 on v2

--- a/solution.py
+++ b/solution.py
@@ -17,8 +17,9 @@
 PLAN = (1, 1, 2, 2)
 
 T0, TP1, TM1, TP2, TM2, U0, UM1, UM2 = range(8)
-PP1, PM1, PP2, PU0, PUM1 = range(5)
-DIRECT = ((TP1, TM1),)
+PP1, PU0 = range(2)
+LATE = ((TM1, -1, False), (UM1, -1, True), (TP2, 2, False))
+DIRECT = ((TM1, TP1), (TM2, TP2))
 
 
 def iota(shape, dim):
@@ -51,14 +52,12 @@
     return out[:rows] + out[rows : 2 * rows] + out[2 * rows :]
 
 
-def kernel(shards, capacity, plan, emb_hbm, cid_hbm, rank_hbm, out_ref, *refs):
+def kernel(shards, capacity, plan, emb_hbm, cid_ref, rank_ref, out_ref, *refs):
     n = len(plan)
     m = n + len(DIRECT)
     send_buf, recv_buf, refs = refs[:m], refs[m : 2 * m], refs[2 * m :]
     (
         emb_ref,
-        cid_ref,
-        rank_ref,
         blk,
         acc,
         meta_send,
@@ -103,14 +102,8 @@
     z, core = grp // 2, grp % 2
     n_z = lax.axis_size("grp") // 2
 
-    loads = [
-        pltpu.make_async_copy(src, dst, in_sem.at[a])
-        for a, (src, dst) in enumerate(
-            ((cid_hbm, cid_ref), (rank_hbm, rank_ref), (emb_hbm, emb_ref))
-        )
-    ]
-    for load in loads:
-        load.start()
+    load = pltpu.make_async_copy(emb_hbm, emb_ref, in_sem)
+    load.start()
 
     def xy_dev(k, sign):
         dy, dx = k // SIDE, k % SIDE
@@ -138,8 +131,6 @@
     def arrived(ref, sem):
         pltpu.make_async_copy(ref, ref, sem).wait()
 
-    loads[0].wait()
-    loads[1].wait()
     cid = cid_ref[...]
     owner = cid // CLUST_OWN
     rel = ((owner // SIDE - y + SIDE) % SIDE) * SIDE + (owner % SIDE - x + SIDE) % SIDE
@@ -160,7 +151,7 @@
     for k in range(1, shards):
         meta_send[k] = meta[k : k + 1]
 
-    loads[2].wait()
+    load.wait()
     wide = emb_ref[...].astype(jnp.float32)
     normed = (
         wide * lax.rsqrt(jnp.sum(wide * wide, axis=1, keepdims=True) + 1e-06)
@@ -190,9 +181,9 @@
 
     pack_chunk(0)
     pl.semaphore_wait(barrier, shards - 1 + len(column))
+    send_chunk(0)
     for k in range(1, shards):
         remote(meta_send.at[k], meta_recv.at[k], meta_ssem, meta_rsem, xy_dev(k, 1))
-    send_chunk(0)
     for b, d in neighbours:
         remote(raw_target.at[T0], raw_target.at[b], rt_send, rt_recv, z_dev(d, False))
         remote(raw.at[T0], raw.at[b], raw_ssem.at[b], raw_rsem.at[b], z_dev(d, False))
@@ -236,28 +227,37 @@
 
     def compact(q):
         units = plan[q]
-        if units not in gathers:
-            gathers[units] = jnp.concatenate([place(units, h) for h in range(units)], axis=0)
+        for h in range(units):
+            if (units, h) not in gathers:
+                gathers[units, h] = place(units, h)
         arrived(recv_buf[q].at[pl.ds(1, shards - 1)], xy_recv.at[q])
         rows = recv_buf[q][...]
-        out = dot_nn(gathers[units], rows.reshape(rows.shape[0] * rows.shape[1], UNIT))
-        blk[T0, first[q] : first[q + 1]] = out.reshape(units, row_dev, UNIT).astype(jnp.bfloat16)
+        rows = rows.reshape(rows.shape[0] * rows.shape[1], UNIT)
+        for h in range(units):
+            blk[T0, first[q] + h] = dot_nn(gathers[units, h], rows).astype(jnp.bfloat16)
+            send_own(first[q] + h)
 
     def direct_places(e):
         places = []
         for h, b in enumerate(DIRECT[e]):
             packed = counts[b][:, :1].astype(jnp.int32)
             places.append(place(2, h, packed % 1024, packed // 1024))
-        return jnp.concatenate(places, axis=0)
+        return places
 
     def compact_direct(e):
         arrived(recv_buf[n + e].at[pl.ds(1, shards - 1)], xy_recv.at[n + e])
         rows = recv_buf[n + e][...]
-        out = dot_nn(
-            direct_gather[e], rows.reshape(rows.shape[0] * rows.shape[1], UNIT)
-        ).astype(jnp.bfloat16)
+        rows = rows.reshape(rows.shape[0] * rows.shape[1], UNIT)
         for h, b in enumerate(DIRECT[e]):
-            blk[b, last] = out[h * row_dev : (h + 1) * row_dev]
+            blk[b, last] = dot_nn(direct_gather[e][h], rows).astype(jnp.bfloat16)
+            if b == TM1:
+                if TM2 not in direct:
+                    z_copy(TM1, TM2, last, 1, False)
+                z_copy(TM1, UM1, last, 0, True)
+            elif b == TP1 and TP2 not in direct:
+                z_copy(TP1, TP2, last, -1, False)
+            elif b == TM2:
+                z_copy(TM2, UM2, last, 0, True)
 
     def z_copy(src_slot, dst_slot, u, d, o):
         remote(
@@ -274,14 +274,11 @@
     def units_of(q):
         return range(first[q], first[q + 1])
 
-    def send_own(q):
-        for u in units_of(q):
-            if u == last:
-                continue
+    def send_own(u):
+        if u != last:
             z_copy(T0, TM1, u, 1, False)
             z_copy(T0, TP1, u, -1, False)
-        for u in units_of(q):
-            z_copy(T0, U0, u, 0, True)
+        z_copy(T0, U0, u, 0, True)
 
     def forward(q):
         for u in units_of(q):
@@ -294,7 +291,6 @@
             z_copy(TP1, TP2, u, -1, False)
 
     compact(0)
-    send_own(0)
 
     member = iota((shards, row_dev), 1)
     from_src = (member >= offset) & (member < offset + count)
@@ -309,7 +305,10 @@
     counts[T0] = jnp.broadcast_to((offset + 1024 * count).astype(jnp.float32), (shards, 128))
     for b, d in neighbours:
         remote(counts.at[T0], counts.at[b], c_send, c_recv, z_dev(d, False))
-    zmeta[T0] = key_row
+    source = jnp.sum(jnp.where(from_src, iota((shards, row_dev), 0), 0), axis=0, keepdims=True)
+    zmeta[T0] = jnp.concatenate(
+        [key_row, source.astype(jnp.float32) * row_dev + home_row], axis=0
+    )
     for slot_no, d, o in (
         (TP1, -1, False),
         (TM1, 1, False),
@@ -325,14 +324,18 @@
         arrived(raw_target.at[pl.ds(1, len(direct))], rt_recv)
     for q in range(1, n):
         compact(q)
-        send_own(q)
         if q <= len(DIRECT):
             pack_direct(q - 1)
         forward(q - 1)
         if q == PREPARE:
             home = one_hot(iota((row_dev, row_dev), 0) == home_row.astype(jnp.int32))
             arrived(zmeta.at[pl.ds(1, 7)], zm_recv)
-            keys = zmeta[...].reshape(8, row_dev)
+            keys = zmeta[:, 0, :]
+            late_src, late_home = [], []
+            for b, _, _ in LATE:
+                code = zmeta[b, 1:2, :].astype(jnp.int32)
+                late_src.append(iota((shards, row_dev), 0) == code // row_dev)
+                late_home.append(one_hot(iota((row_dev, row_dev), 0) == code % row_dev))
             eye = one_hot(iota((row_dev, row_dev), 0) == iota((row_dev, row_dev), 1), jnp.float32)
             keys_t = dot_nt(eye, keys, HIGHEST)
             for b in range(8):
@@ -344,10 +347,6 @@
     forward(n - 1)
     if DIRECT:
         compact_direct(0)
-        z_copy(TM1, UM1, last, 0, True)
-        if TM2 not in direct:
-            z_copy(TM1, TM2, last, 1, False)
-            z_copy(TP1, TP2, last, -1, False)
 
     def scores(query, key, start, stop):
         total = None
@@ -394,10 +393,30 @@
         z_wait(UM1, u)
     send_part(PP1, jnp.maximum(early_p1, best(TP1, (UM1,))), 1, False)
     early_um1 = best(UM1, (TP1,))
+
+    def give_back(group, value, chosen, rows, d, o):
+        back = dot_whole(jnp.where(chosen, value, 0.0), rows)
+        ret_send[group] = back.reshape(shards, 1, row_dev)
+        for k in range(shards):
+            if group == 0 and k == 0:
+                continue
+            plane, _ = xy_dev(k, -1)
+            remote(
+                ret_send.at[group, k],
+                ret_recv.at[group, k],
+                r_send.at[group],
+                r_recv.at[group],
+                (plane, z_dev(d, o)[1]),
+            )
+        if group == 0:
+            ret_recv[0, 0] = back[0:1]
+
+    def give_late(group, value):
+        _, d, o = LATE[group - 1]
+        give_back(group, value, late_src[group - 1], late_home[group - 1], d, o)
     pass_on(range(first[n - 2], tail))
     if len(DIRECT) > 1:
         compact_direct(1)
-        z_copy(TM2, UM2, last, 0, True)
 
     for u in range(tail):
         z_wait(TP2, u)
@@ -416,23 +435,24 @@
     pass_on(by_z)
     for u in by_z:
         z_wait(TP2, u)
-    send_part(PM1, jnp.maximum(early_m1, finish(0)), -1, False)
-    send_part(PUM1, jnp.maximum(early_um1, finish(1)), -1, True)
+    late_m1 = jnp.maximum(early_m1, finish(0))
+    late_um1 = jnp.maximum(early_um1, finish(1))
     late = jnp.maximum(jnp.maximum(finish(2), finish(3)), finish(4))
     for u in range(tail, first[n]):
         z_wait(UM2, u)
-    send_part(PP2, jnp.maximum(late, finish(5)), 2, False)
+    give_late(3, jnp.maximum(late, finish(5)))
+    give_late(1, late_m1)
+    give_late(2, late_um1)
 
     arrived(part_recv, p_recv)
-    mine = jnp.maximum(mine, jnp.max(part_recv[...].reshape(5, row_dev), axis=0, keepdims=True))
-    back = dot_whole(jnp.where(from_src, mine, 0.0), home)
-    ret_recv[0] = back[0:1]
-    for k in range(1, shards):
-        ret_send[k] = back[k : k + 1]
-    for k in range(1, shards):
-        remote(ret_send.at[k], ret_recv.at[k], r_send, r_recv, xy_dev(k, -1))
-    arrived(ret_recv.at[pl.ds(1, shards - 1)], r_recv)
-    out_ref[...] = jnp.sum(ret_recv[...].reshape(shards, row_dev), axis=0, keepdims=True)
+    mine = jnp.maximum(mine, jnp.max(part_recv[...].reshape(2, row_dev), axis=0, keepdims=True))
+    give_back(0, mine, from_src, home, 0, False)
+
+    arrived(ret_recv.at[0, pl.ds(1, shards - 1)], r_recv.at[0])
+    for group in range(1, 1 + len(LATE)):
+        arrived(ret_recv.at[group], r_recv.at[group])
+    found = jnp.sum(ret_recv[...].reshape(1 + len(LATE), shards, row_dev), axis=1)
+    out_ref[...] = jnp.max(found, axis=0, keepdims=True)
 
     arrived(meta_send.at[pl.ds(1, shards - 1)], meta_ssem)
     for q in range(m):
@@ -450,7 +470,9 @@
         arrived(counts.at[pl.ds(1, len(direct))], c_send)
     arrived(zmeta.at[pl.ds(1, 7)], zm_send)
     arrived(part_send, p_send)
-    arrived(ret_send.at[pl.ds(1, shards - 1)], r_send)
+    arrived(ret_send.at[0, pl.ds(1, shards - 1)], r_send.at[0])
+    for group in range(1, 1 + len(LATE)):
+        arrived(ret_send.at[group], r_send.at[group])
 
 
 def per_device(embedding, cluster_id, member_order):
@@ -462,7 +484,7 @@
     n = len(plan)
     dma = pltpu.SemaphoreType.DMA
     vmem = pltpu.VMEM
-    bf16, f32, i32 = jnp.bfloat16, jnp.float32, jnp.int32
+    bf16, f32 = jnp.bfloat16, jnp.float32
     messages = [
         vmem((shards, padded if units == 1 else units * capacity, UNIT), bf16)
         for units in plan + (2,) * len(DIRECT)
@@ -470,28 +492,26 @@
     out = pl.pallas_call(
         functools.partial(kernel, shards, capacity, plan),
         out_shape=jax.ShapeDtypeStruct((1, row_dev), f32),
-        in_specs=[pl.BlockSpec(memory_space=pltpu.HBM)] * 3,
+        in_specs=[pl.BlockSpec(memory_space=pltpu.HBM)] + [pl.BlockSpec(memory_space=vmem)] * 2,
         out_specs=pl.BlockSpec(memory_space=vmem),
         scratch_shapes=messages
         + messages
         + [
             vmem((row_dev, depth), bf16),
-            vmem((1, row_dev), i32),
-            vmem((1, row_dev), i32),
             vmem((8, depth // UNIT, row_dev, UNIT), bf16),
             vmem((6, row_dev, row_dev), f32),
             vmem((shards, 1, 128), f32),
             vmem((shards, 1, 128), f32),
-            vmem((8, 1, row_dev), f32),
+            vmem((8, 2, row_dev), f32),
             vmem((5, row_dev, UNIT), bf16),
             vmem((5, 1, row_dev), f32),
             vmem((5, shards, 128), f32),
             vmem((8, row_dev, 128), f32),
-            vmem((5, 1, row_dev), f32),
-            vmem((5, 1, row_dev), f32),
-            vmem((shards, 1, row_dev), f32),
-            vmem((shards, 1, row_dev), f32),
-            dma((3,)),
+            vmem((2, 1, row_dev), f32),
+            vmem((2, 1, row_dev), f32),
+            vmem((1 + len(LATE), shards, 1, row_dev), f32),
+            vmem((1 + len(LATE), shards, 1, row_dev), f32),
+            dma,
             dma((n + len(DIRECT),)),
             dma((n + len(DIRECT),)),
             dma,
@@ -508,8 +528,8 @@
             dma,
             dma,
             dma,
-            dma,
-            dma,
+            dma((1 + len(LATE),)),
+            dma((1 + len(LATE),)),
         ],
         compiler_params=pltpu.CompilerParams(
             collective_id=0, has_side_effects=True, vmem_limit_bytes=215 * 2**18

time: 46.9 us -> 44.8 us (0.955)
  Pallas kernels: 45.1 us -> 43.4 us
    pallas_call x1, Pallas kernels: 45.1 us -> 43.4 us  [per_device(): pl.pallas_call(functools.partial(kernel, shards, capacity, plan), out_sha...]
where the time goes in v3:
time: 44.8 us; the launch traced here: 44.7 us
  Pallas kernels  43.4 us (97%)
  local copies, waits for them, and re-layouts  1.26 us (3%)
    pallas_call x1, Pallas kernels, per_device(): pl.pallas_call(functools.partial(kernel, shards, capacity, plan), out_sha...  43.4 us
    unnamed x5, local copies, waits for them, and re-layouts  1.26 us

profile of v3, /device:TPU:1, one launch (start us, length us, event | category | flops | bytes accessed | tf_op | source)
XLA Modules:
  0.0 44.7 jit_solution(5885258133897095287)
XLA Ops:
  0.0 0.0 copy-start.1
  0.0 0.0 copy-start
  0.0 0.7 %copy-done.1 = s32[256]{0:T(256)S(1)} copy-done((s32[256]{0:T(256)S(1)}, s32[256]{0:T(256)}, u32[]{:S(2)}) %copy-start.1) | copy-done | bytes 1048
  0.7 0.0 copy-done
  0.7 43.4 %shard_map.37 = f32[1,256]{1,0:T(1,128)S(1)} custom-call(bf16[256,768]{1,0:T(8,128)(2,1)} %emb_hbm.1, s32[1,256]{1,0:T(1,128)S(1)} %bitcast.4, s32[1,256]{1,0:T(1,128)S(1)} %bitcast.5), custom_call_target="tpu_custom_call" | custom-call | tf_op jit(solution)/shard_map/pallas_call | solution.py:492
  44.1 0.6 %copy.5 = f32[256]{0:T(256)} copy(f32[256]{0:T(256)S(1)} %bitcast.3) | data formatting | bytes 2048
Async XLA Ops:
  0.0 0.7 %copy-start.1 = (s32[256]{0:T(256)S(1)}, s32[256]{0:T(256)}, u32[]{:S(2)}) copy-start(s32[256]{0:T(256)} %param.5) | copy-start | bytes 3076
  0.0 0.7 %copy-start = (s32[256]{0:T(256)S(1)}, s32[256]{0:T(256)}, u32[]{:S(2)}) copy-start(s32[256]{0:T(256)} %param.4) | copy-start | bytes 3076

commit v4 on v3

--- a/solution.py
+++ b/solution.py
@@ -344,9 +344,9 @@
             if DIRECT:
                 arrived(counts.at[pl.ds(1, len(direct))], c_recv)
             direct_gather = [direct_places(e) for e in range(len(DIRECT))]
-    forward(n - 1)
     if DIRECT:
         compact_direct(0)
+    forward(n - 1)
 
     def scores(query, key, start, stop):
         total = None

time: 44.8 us -> 44.3 us (0.989)
  Pallas kernels: 43.4 us -> 42.9 us
    pallas_call x1, Pallas kernels: 43.4 us -> 42.9 us  [per_device(): pl.pallas_call(functools.partial(kernel, shards, capacity, plan), out_sha...]
where the time goes in v4:
time: 44.3 us; the launch traced here: 44.2 us
  Pallas kernels  42.9 us (97%)
  local copies, waits for them, and re-layouts  1.26 us (3%)
    pallas_call x1, Pallas kernels, per_device(): pl.pallas_call(functools.partial(kernel, shards, capacity, plan), out_sha...  42.9 us
    unnamed x5, local copies, waits for them, and re-layouts  1.26 us

profile of v4, /device:TPU:1, one launch (start us, length us, event | category | flops | bytes accessed | tf_op | source)
XLA Modules:
  0.0 44.2 jit_solution(18324820172380694123)
XLA Ops:
  0.0 0.0 copy-start.1
  0.0 0.0 copy-start
  0.0 0.7 %copy-done.1 = s32[256]{0:T(256)S(1)} copy-done((s32[256]{0:T(256)S(1)}, s32[256]{0:T(256)}, u32[]{:S(2)}) %copy-start.1) | copy-done | bytes 1048
  0.7 0.0 copy-done
  0.7 42.9 %shard_map.37 = f32[1,256]{1,0:T(1,128)S(1)} custom-call(bf16[256,768]{1,0:T(8,128)(2,1)} %emb_hbm.1, s32[1,256]{1,0:T(1,128)S(1)} %bitcast.4, s32[1,256]{1,0:T(1,128)S(1)} %bitcast.5), custom_call_target="tpu_custom_call" | custom-call | tf_op jit(solution)/shard_map/pallas_call | solution.py:492
  43.6 0.6 %copy.5 = f32[256]{0:T(256)} copy(f32[256]{0:T(256)S(1)} %bitcast.3) | data formatting | bytes 2048
Async XLA Ops:
  0.0 0.7 %copy-start.1 = (s32[256]{0:T(256)S(1)}, s32[256]{0:T(256)}, u32[]{:S(2)}) copy-start(s32[256]{0:T(256)} %param.5) | copy-start | bytes 3076
  0.0 0.7 %copy-start = (s32[256]{0:T(256)S(1)}, s32[256]{0:T(256)}, u32[]{:S(2)}) copy-start(s32[256]{0:T(256)} %param.4) | copy-start | bytes 3076

commit v5 on v4

--- a/solution.py
+++ b/solution.py
@@ -173,8 +173,12 @@
         recv_buf[q][0] = rows[0]
         send_buf[q][1:] = rows[1:]
 
+    def hops(k):
+        dy, dx = k // SIDE, k % SIDE
+        return min(dy, SIDE - dy) + min(dx, SIDE - dx)
+
     def send_chunk(q):
-        for k in range(1, shards):
+        for k in sorted(range(1, shards), key=hops, reverse=True):
             remote(
                 send_buf[q].at[k], recv_buf[q].at[k], xy_send.at[q], xy_recv.at[q], xy_dev(k, 1)
             )
@@ -397,7 +401,7 @@
     def give_back(group, value, chosen, rows, d, o):
         back = dot_whole(jnp.where(chosen, value, 0.0), rows)
         ret_send[group] = back.reshape(shards, 1, row_dev)
-        for k in range(shards):
+        for k in sorted(range(shards), key=hops, reverse=True):
             if group == 0 and k == 0:
                 continue
             plane, _ = xy_dev(k, -1)

time: 44.3 us -> 44.5 us (level)
  no operation moved by 1% of the time
where the time goes in v5:
time: 44.5 us; the launch traced here: 44.3 us
  Pallas kernels  43.1 us (97%)
  local copies, waits for them, and re-layouts  1.26 us (3%)
    pallas_call x1, Pallas kernels, per_device(): pl.pallas_call(functools.partial(kernel, shards, capacity, plan), out_sha...  43.1 us
    unnamed x5, local copies, waits for them, and re-layouts  1.26 us

profile of v5, /device:TPU:1, one launch (start us, length us, event | category | flops | bytes accessed | tf_op | source)
XLA Modules:
  0.0 44.3 jit_solution(11553486509422492739)
XLA Ops:
  0.0 0.0 copy-start.1
  0.0 0.0 copy-start
  0.0 0.7 %copy-done.1 = s32[256]{0:T(256)S(1)} copy-done((s32[256]{0:T(256)S(1)}, s32[256]{0:T(256)}, u32[]{:S(2)}) %copy-start.1) | copy-done | bytes 1048
  0.7 0.0 copy-done
  0.7 43.1 %shard_map.37 = f32[1,256]{1,0:T(1,128)S(1)} custom-call(bf16[256,768]{1,0:T(8,128)(2,1)} %emb_hbm.1, s32[1,256]{1,0:T(1,128)S(1)} %bitcast.4, s32[1,256]{1,0:T(1,128)S(1)} %bitcast.5), custom_call_target="tpu_custom_call" | custom-call | tf_op jit(solution)/shard_map/pallas_call | solution.py:496
  43.8 0.6 %copy.5 = f32[256]{0:T(256)} copy(f32[256]{0:T(256)S(1)} %bitcast.3) | data formatting | bytes 2048
Async XLA Ops:
  0.0 0.7 %copy-start.1 = (s32[256]{0:T(256)S(1)}, s32[256]{0:T(256)}, u32[]{:S(2)}) copy-start(s32[256]{0:T(256)} %param.5) | copy-start | bytes 3076
  0.0 0.7 %copy-start = (s32[256]{0:T(256)S(1)}, s32[256]{0:T(256)}, u32[]{:S(2)}) copy-start(s32[256]{0:T(256)} %param.4) | copy-start | bytes 3076

commit v6 on v4

--- a/solution.py
+++ b/solution.py
@@ -324,8 +324,9 @@
         arrived(raw_target.at[pl.ds(1, len(direct))], rt_recv)
     for q in range(1, n):
         compact(q)
-        if q <= len(DIRECT):
-            pack_direct(q - 1)
+        if q == 1:
+            for e in range(len(DIRECT)):
+                pack_direct(e)
         forward(q - 1)
         if q == PREPARE:
             home = one_hot(iota((row_dev, row_dev), 0) == home_row.astype(jnp.int32))

time: 44.3 us -> 44.3 us (level)
  no operation moved by 1% of the time
where the time goes in v6:
time: 44.3 us; the launch traced here: 44.2 us
  Pallas kernels  42.9 us (97%)
  local copies, waits for them, and re-layouts  1.26 us (3%)
    pallas_call x1, Pallas kernels, per_device(): pl.pallas_call(functools.partial(kernel, shards, capacity, plan), out_sha...  42.9 us
    unnamed x5, local copies, waits for them, and re-layouts  1.26 us

profile of v6, /device:TPU:1, one launch (start us, length us, event | category | flops | bytes accessed | tf_op | source)
XLA Modules:
  0.0 44.2 jit_solution(2590283790881410523)
XLA Ops:
  0.0 0.0 copy-start.1
  0.0 0.0 copy-start
  0.0 0.7 %copy-done.1 = s32[256]{0:T(256)S(1)} copy-done((s32[256]{0:T(256)S(1)}, s32[256]{0:T(256)}, u32[]{:S(2)}) %copy-start.1) | copy-done | bytes 1048
  0.7 0.0 copy-done
  0.7 42.9 %shard_map.37 = f32[1,256]{1,0:T(1,128)S(1)} custom-call(bf16[256,768]{1,0:T(8,128)(2,1)} %emb_hbm.1, s32[1,256]{1,0:T(1,128)S(1)} %bitcast.4, s32[1,256]{1,0:T(1,128)S(1)} %bitcast.5), custom_call_target="tpu_custom_call" | custom-call | tf_op jit(solution)/shard_map/pallas_call | solution.py:493
  43.6 0.6 %copy.5 = f32[256]{0:T(256)} copy(f32[256]{0:T(256)S(1)} %bitcast.3) | data formatting | bytes 2048
Async XLA Ops:
  0.0 0.7 %copy-start.1 = (s32[256]{0:T(256)S(1)}, s32[256]{0:T(256)}, u32[]{:S(2)}) copy-start(s32[256]{0:T(256)} %param.5) | copy-start | bytes 3076
  0.0 0.7 %copy-start = (s32[256]{0:T(256)S(1)}, s32[256]{0:T(256)}, u32[]{:S(2)}) copy-start(s32[256]{0:T(256)} %param.4) | copy-start | bytes 3076
